TPU v7x, 512 devices: a whole 4x8x8 slice. The times are simulated.
512 devices in a mesh: expert: 8 (over x, core), tensor: 64 (over y, z).
Axes of the slice: x: 4, y: 8, z: 8, core: 2. Of those that a mesh axis runs over, the one named last changes fastest.
Arguments:
- tokens: bfloat16 [384, 3072], P('expert', 'tensor'), may hold values from -6 to 6
- cotangent: bfloat16 [384, 3072], P('expert', 'tensor'), may hold values from -6 to 6
- routes: int32 [384, 2], P('expert'), may hold values from 0 to 7, all different within a row; in each aligned block of 48 rows (0 to 47, 48 to 95, ...) at most 20 rows name the same one
- route_weight: float32 [384, 2], P('expert'), may hold values from 0.1 to 1
- w_gate: bfloat16 [8, 3072, 16384], P('expert', None, 'tensor'), may hold values from -0.109375 to 0.109375
- w_up: bfloat16 [8, 3072, 16384], P('expert', None, 'tensor'), may hold values from -0.109375 to 0.109375
- w_down: bfloat16 [8, 16384, 3072], P('expert', 'tensor'), may hold values from -0.125 to 0.125
Outputs:
- mixed: bfloat16 [384, 3072], P('expert', 'tensor')
- input_grad: bfloat16 [384, 3072], P('expert', 'tensor')
Inputs may be any that keep to these rules, and one draw needn't show every extreme that they name: `routes`: the two experts of a token differ. Among the 48 tokens of one index of the expert axis, no expert is named by more than 20 of them, and in every draw some expert is named by exactly 20 of them in some such block.
All inputs are finite; a program needn't handle non-finite values.
Results may differ from a plain program's by a relative error of at most 0.0057.
Values may be sent and summed in bfloat16 or wider, within the bound.
A program may use at most 64 MiB of HBM per device.

v0:
```python
import jax
import jax.numpy as jnp
from jax import lax
from jax.sharding import PartitionSpec as P


def swish_parts(gate_pre):
    sigma_gate = jax.nn.sigmoid(gate_pre)
    return (sigma_gate, gate_pre * sigma_gate)


def contract_first(left, right):
    return lax.dot_general(
        left, right, (((0,), (0,)), ((), ())), preferred_element_type=jnp.float32
    )


def contract_pairs(left, right):
    return lax.dot_general(
        left, right, (((0, 1), (0, 1)), ((), ())), preferred_element_type=jnp.float32
    )


def contract_last(left, right):
    return lax.dot_general(
        left, right, (((1,), (1,)), ((), ())), preferred_element_type=jnp.float32
    )


def shards(tokens, cotangent, routes, route_weight, w_gate, w_up, w_down):
    group_count = lax.axis_size("expert")
    tok_rows = tokens.shape[0]
    top_count = routes.shape[1]
    capacity = min(tok_rows, tok_rows * 10 // (3 * group_count))
    slot_rows = group_count * capacity
    gate_mat = w_gate[0]
    up_mat = w_up[0]
    down_mat = w_down[0]
    one_hot = (
        routes[:, :, None] == jnp.arange(group_count, dtype=jnp.int32)[None, None, :]
    ).astype(jnp.int32)
    flattened = one_hot.reshape(tok_rows * top_count, group_count)
    earlier = jnp.cumsum(flattened, axis=0) - flattened
    position = jnp.sum(earlier * flattened, axis=1).reshape(tok_rows, top_count)
    target_row = routes * capacity + position
    matches = (
        target_row[:, :, None] == jnp.arange(slot_rows, dtype=jnp.int32)[None, None, :]
    ).astype(jnp.bfloat16)
    placing_low = jnp.sum(matches, axis=1)
    flat_targets = target_row.reshape(tok_rows * top_count)
    send_tokens = contract_first(placing_low, tokens).astype(jnp.bfloat16)
    send_grads = contract_pairs(
        matches,
        (route_weight[:, :, None] * cotangent.astype(jnp.float32)[:, None, :]).astype(jnp.bfloat16),
    ).astype(jnp.bfloat16)
    recv_tokens, recv_grads = (
        lax.all_to_all(send_tokens, "expert", split_axis=0, concat_axis=0, tiled=True),
        lax.all_to_all(send_grads, "expert", split_axis=0, concat_axis=0, tiled=True),
    )
    piece_tokens = lax.all_gather(recv_tokens, "tensor", axis=1, tiled=True)
    piece_grads = lax.all_gather(recv_grads, "tensor", axis=1, tiled=True)
    gate_pre = jnp.dot(piece_tokens, gate_mat, preferred_element_type=jnp.float32)
    up_pre = jnp.dot(piece_tokens, up_mat, preferred_element_type=jnp.float32)
    grad_hidden = contract_last(piece_grads, down_mat)
    sigma_gate, swish = swish_parts(gate_pre)
    hidden = (swish * up_pre).astype(jnp.bfloat16)
    expert_out = jnp.dot(hidden, down_mat, preferred_element_type=jnp.float32)
    grad_gate = (grad_hidden * up_pre * sigma_gate * (1.0 + gate_pre * (1.0 - sigma_gate))).astype(
        jnp.bfloat16
    )
    grad_up = (grad_hidden * swish).astype(jnp.bfloat16)
    grad_input = contract_last(grad_gate, gate_mat) + contract_last(grad_up, up_mat)
    summed_out, summed_grad = (
        lax.psum_scatter(expert_out, "tensor", scatter_dimension=1, tiled=True),
        lax.psum_scatter(grad_input, "tensor", scatter_dimension=1, tiled=True),
    )
    back_out, back_grad = (
        lax.all_to_all(summed_out, "expert", split_axis=0, concat_axis=0, tiled=True),
        lax.all_to_all(summed_grad, "expert", split_axis=0, concat_axis=0, tiled=True),
    )
    width = back_out.shape[1]
    out_pairs = jnp.take(back_out, flat_targets, axis=0).reshape(tok_rows, top_count, width)
    grad_pairs = jnp.take(back_grad, flat_targets, axis=0).reshape(tok_rows, top_count, width)
    mixed_out = jnp.sum(route_weight[:, :, None] * out_pairs, axis=1)
    input_out = jnp.sum(grad_pairs, axis=1)
    return (mixed_out.astype(jnp.bfloat16), input_out.astype(jnp.bfloat16))


def solution(mesh):
    return jax.shard_map(
        shards,
        mesh=mesh,
        in_specs=(
            P("expert", "tensor"),
            P("expert", "tensor"),
            P("expert", None),
            P("expert", None),
            P("expert", None, "tensor"),
            P("expert", None, "tensor"),
            P("expert", "tensor", None),
        ),
        out_specs=(P("expert", "tensor"), P("expert", "tensor")),
        check_vma=False,
    )
```

profile of v0, /device:TPU:1, one launch (start us, length us, event | category | flops | bytes accessed | tf_op | source)
XLA Modules:
  0.0 650.6 jit_solution(17949297718436534936)
XLA Ops:
  7.2 0.0 copy-start
  7.2 0.9 copy.40
  8.1 0.1 eq.29
  8.2 0.1 fusion.17
  8.3 0.1 reduce_window_sum.11
  8.4 0.2 select_reduce_fusion
  8.6 0.1 reshape.36
  8.7 0.1 copy.41
  8.8 0.7 multiply_add_fusion
  9.5 0.1 fusion.15
  9.6 0.9 convolution_convert_fusion
  10.5 0.1 copy.43
  10.6 0.7 reshape.63
  11.3 10.1 %all-to-all-start = ((bf16[8,2,480]{2,1,0:T(2,128)(2,1)}), bf16[8,2,480]{2,1,0:T(2,128)(2,1)S(1)}, u32[]{:S(2)}, u32[]{:S(2)}) async-start(bf16[8,2,480]{2,1,0:T(2,128)(2,1)} %reshape.63), calls=%async_computation | async-start | bytes 32768 | tf_op jit(solution)/shard_map/all_to_all | solution.py:57
  21.5 0.8 copy.47
  22.2 0.9 fusion.11
  23.1 0.1 copy.48
  23.3 0.7 reshape.67
  24.0 2.1 all-to-all-done
  26.1 3.9 all-to-all-start.2
  30.1 0.1 reshape.64
  30.2 0.1 copy.44
  30.3 43.4 %all_gather.6 = bf16[160,3072]{0,1:T(8,128)(2,1)S(1)} all-gather(bf16[160,48]{0,1:T(8,128)(2,1)S(1)} %copy.44), channel_id=1, replica_groups=mesh['expert'=8,'tensor'=64] {'tensor'}, dimensions={1}, use_global_device_ids=true | all-gather | bytes 998400 | tf_op jit(solution)/shard_map/all_gather | solution.py:60
  73.7 0.0 copy-start.2
  73.7 0.6 fusion.9
  74.3 0.8 copy-done.2
  75.1 0.6 fusion.5
  75.7 0.0 copy-start.1
  75.7 0.1 reshape.68
  75.8 0.6 all_to_all.40
  76.4 0.9 copy.49
  77.3 36.6 %all_gather.7 = bf16[160,3072]{0,1:T(8,128)(2,1)S(1)} all-gather(bf16[160,48]{0,1:T(8,128)(2,1)S(1)} %copy.49), channel_id=1, replica_groups=mesh['expert'=8,'tensor'=64] {'tensor'}, dimensions={1}, use_global_device_ids=true | all-gather | bytes 998400 | tf_op jit(solution)/shard_map/all_gather | solution.py:61
  113.9 0.7 fusion
  114.6 0.0 copy-start.3
  114.7 0.6 fusion.7
  115.3 0.8 copy-done.3
  116.1 2.3 convolution_add_fusion
  118.4 0.0 reduce-scatter.5.cloned.1.call-update
  118.4 0.0 reduce-scatter.3.cloned.1.call-start
  118.4 2.4 fusion.2
  120.9 0.0 reduce-scatter.3.cloned.1.call-update
  120.9 0.0 copy-start.4
  120.9 0.1 copy.42
  121.0 0.1 reshape.37
  121.1 256.2 %reduce-scatter.5.cloned.1.call-done = f32[160,48]{0,1:T(8,128)} async-done(((f32[160,3072]{0,1:T(8,128)}), f32[160,48]{0,1:T(8,128)}) %reduce-scatter.5.cloned.1.call-update) | async-done | bytes 30736 | tf_op jit(solution)/shard_map/reduce_scatter | solution.py:75
  377.3 0.9 copy.50
  378.2 0.7 reshape.69
  378.9 9.7 %all-to-all-start.3 = ((f32[8,1,960]{2,1,0:T(1,128)}), f32[8,1,960]{2,1,0:T(1,128)S(1)}, u32[]{:S(2)}, u32[]{:S(2)}) async-start(f32[8,1,960]{2,1,0:T(1,128)} %reshape.69), calls=%async_computation.5 | async-start | bytes 65536 | tf_op jit(solution)/shard_map/all_to_all | solution.py:79
  388.6 235.5 %reduce-scatter.3.cloned.1.call-done = f32[160,48]{0,1:T(8,128)} async-done(((f32[160,3072]{0,1:T(8,128)}), f32[160,48]{0,1:T(8,128)}) %reduce-scatter.3.cloned.1.call-update) | async-done | bytes 30736 | tf_op jit(solution)/shard_map/reduce_scatter | solution.py:74
  624.1 0.9 copy.45
  625.0 0.7 reshape.65
  625.7 9.7 %all-to-all-start.1 = ((f32[8,1,960]{2,1,0:T(1,128)}), f32[8,1,960]{2,1,0:T(1,128)S(1)}, u32[]{:S(2)}, u32[]{:S(2)}) async-start(f32[8,1,960]{2,1,0:T(1,128)} %reshape.65), calls=%async_computation.2 | async-start | bytes 65536 | tf_op jit(solution)/shard_map/all_to_all | solution.py:78
  635.4 0.5 broadcast.34
  635.9 0.7 reduce.1
  636.6 0.1 reshape.70
  636.7 3.4 all-to-all-done.1
  640.1 0.7 reduce.2
  640.8 0.1 reshape.66
  640.9 0.6 gather_fusion.1
  641.6 0.6 gather_fusion
  642.2 0.1 broadcast_select_fusion
  642.3 0.1 copy.46
  642.4 0.7 copy.51
  643.1 0.7 reduce_sum.42
  (17 shorter events, 0.1 us)
Async XLA Ops:
  7.2 66.5 %copy-start = (bf16[1,3072,256]{2,1,0:T(8,128)(2,1)S(1)}, bf16[1,3072,256]{2,1,0:T(8,128)(2,1)}, u32[]{:S(2)}) copy-start(bf16[1,3072,256]{2,1,0:T(8,128)(2,1)} %param.13) | copy-start | bytes 4718596
  11.3 14.8 %all-to-all-start = ((bf16[8,2,480]{2,1,0:T(2,128)(2,1)}), bf16[8,2,480]{2,1,0:T(2,128)(2,1)S(1)}, u32[]{:S(2)}, u32[]{:S(2)}) async-start(bf16[8,2,480]{2,1,0:T(2,128)(2,1)} %reshape.63), calls=%async_computation | async-start | bytes 32768 | tf_op jit(solution)/shard_map/all_to_all | solution.py:57
  26.1 49.5 %all-to-all-start.2 = ((bf16[8,2,480]{2,1,0:T(2,128)(2,1)}), bf16[8,2,480]{2,1,0:T(2,128)(2,1)S(1)}, u32[]{:S(2)}, u32[]{:S(2)}) async-start(bf16[8,2,480]{2,1,0:T(2,128)(2,1)} %reshape.67), calls=%async_computation.3 | async-start | bytes 32768 | tf_op jit(solution)/shard_map/all_to_all | solution.py:58
  30.1 347.2 %reduce-scatter.5.cloned.1.call-start = ((), (), s32[]{:S(2)}) async-start(), calls=%async_computation.7 | async-start | bytes 3194880 | tf_op jit(solution)/shard_map/reduce_scatter | solution.py:75
  73.7 1.4 copy-start.2
  75.7 38.3 %copy-start.1 = (bf16[1,256,3072]{2,1,0:T(8,128)(2,1)S(1)}, bf16[1,256,3072]{2,1,0:T(8,128)(2,1)}, u32[]{:S(2)}) copy-start(bf16[1,256,3072]{2,1,0:T(8,128)(2,1)} %param.15) | copy-start | bytes 4718596
  114.6 1.4 copy-start.3
  118.4 505.7 %reduce-scatter.3.cloned.1.call-start = ((), (), s32[]{:S(2)}) async-start(), calls=%async_computation.6 | async-start | bytes 3194880 | tf_op jit(solution)/shard_map/reduce_scatter | solution.py:74
  120.9 521.5 %copy-start.4 = (f32[48,2]{0,1:T(2,128)S(1)}, f32[48,2]{0,1:T(2,128)}, u32[]{:S(2)}) copy-start(f32[48,2]{0,1:T(2,128)} %param.12) | copy-start | bytes 1156
  378.9 246.8 %all-to-all-start.3 = ((f32[8,1,960]{2,1,0:T(1,128)}), f32[8,1,960]{2,1,0:T(1,128)S(1)}, u32[]{:S(2)}, u32[]{:S(2)}) async-start(f32[8,1,960]{2,1,0:T(1,128)} %reshape.69), calls=%async_computation.5 | async-start | bytes 65536 | tf_op jit(solution)/shard_map/all_to_all | solution.py:79
  625.7 14.4 %all-to-all-start.1 = ((f32[8,1,960]{2,1,0:T(1,128)}), f32[8,1,960]{2,1,0:T(1,128)S(1)}, u32[]{:S(2)}, u32[]{:S(2)}) async-start(f32[8,1,960]{2,1,0:T(1,128)} %reshape.65), calls=%async_computation.2 | async-start | bytes 65536 | tf_op jit(solution)/shard_map/all_to_all | solution.py:78
Sparse Core Ops, SparseCore 0:
  118.5 258.7 reduce-scatter.4
  381.3 242.6 reduce-scatter.2
where the time goes:
time: 651 us
  waiting for transfers between devices  497 us (76%)
  blocking collectives  80 us (12%)
  starting transfers between devices  33.4 us (5%)
  between operations  14.3 us (2%)
  local copies, waits for them, and re-layouts  13.3 us (2%)
  matrix products  8.97 us (1%)
    reduce_scatter x1, waiting for transfers between devices, shards(): lax.psum_scatter(grad_input, 'tensor', scatter_dimension=1, tiled=True)  256 us
    reduce_scatter x1, waiting for transfers between devices, shards(): lax.psum_scatter(expert_out, 'tensor', scatter_dimension=1, tiled=True)  235 us
    all_gather x1, blocking collectives, shards(): piece_tokens = lax.all_gather(recv_tokens, 'tensor', axis=1, tiled=True)  43.4 us
    all_gather x1, blocking collectives, shards(): piece_grads = lax.all_gather(recv_grads, 'tensor', axis=1, tiled=True)  36.6 us
  transfers between devices with their start and end apart: 6, of which 4 were waited for; matrix products, arithmetic and copies ran while one was open for 2% of the time, Pallas kernels for 0%

commit v1 on v0

v1 whole, which is shorter than its diff:
```python
import functools

import jax
import jax.numpy as jnp
from jax import lax
from jax.experimental import pallas as pl
from jax.experimental.pallas import tpu as pltpu
from jax.sharding import PartitionSpec as P

MESH = pl.DeviceIdType.MESH
BF = jnp.bfloat16
F32 = jnp.float32

GROUPS = 8
SIDE = 8
TOK = 48
CAP = 20
PAD = 32
ROWS = GROUPS * CAP
HALF = ROWS // 2
WIDE = SIDE * TOK
HID = 256
LANES = 128
HIGH = 64
ORDER = (1, 7, 2, 6, 3, 5, 4)


def iota(shape, dim):
    return lax.broadcasted_iota(jnp.int32, shape, dim)


def onehot(cond):
    return jnp.where(cond, 1.0, 0.0).astype(BF)


def mm(a, b):
    return lax.dot_general(a, b, (((1,), (0,)), ((), ())), preferred_element_type=F32)


def mm_tn(a, b):
    return lax.dot_general(a, b, (((0,), (0,)), ((), ())), preferred_element_type=F32)


def mm_nt(a, b):
    return lax.dot_general(a, b, (((1,), (1,)), ((), ())), preferred_element_type=F32)


def kernel(
    tok, cot, routes, rw, wg, wu, wd,
    mixed, gin,
    wgu, wdv, plo, phi, dsend, drecv,
    t1, g1, t2, g2, ms, gs, mr, gr, mp, gp, mq, gq, rsend, rrecv,
    wsem, dss, drs, s1, r1, s2, r2, s3, r3, s4, r4, rss, rrs,
):
    e = lax.axis_index("expert")
    t = lax.axis_index("tensor")
    y = t // SIDE
    z = t % SIDE

    def at_e(d):
        return ((e + d) % GROUPS, t)

    def at_y(d):
        return (e, ((y + d) % SIDE) * SIDE + z)

    def at_z(d):
        return (e, y * SIDE + (z + d) % SIDE)

    loads = []
    for k in range(SIDE):
        loads.append(pltpu.make_async_copy(wg.at[:, k], wgu.at[k, :, :, pl.ds(0, HID)], wsem.at[k]))
        loads.append(pltpu.make_async_copy(wu.at[:, k], wgu.at[k, :, :, pl.ds(HID, HID)], wsem.at[SIDE + k]))
    loads.append(pltpu.make_async_copy(wd, wdv, wsem.at[2 * SIDE]))
    for c in loads:
        c.start()

    bar = pltpu.get_barrier_semaphore()
    for at in (at_e, at_y, at_z):
        for d in range(1, 8):
            pl.semaphore_signal(bar, inc=1, device_id=at(d), device_id_type=MESH)

    def send(src, dst, ss, rs, where):
        c = pltpu.make_async_remote_copy(
            src_ref=src, dst_ref=dst, send_sem=ss, recv_sem=rs, device_id=where, device_id_type=MESH
        )
        c.start()
        return c

    r0, r1_ = routes[:, 0:1], routes[:, 1:2]
    w0, w1 = rw[:, 0:1], rw[:, 1:2]
    lane = iota((TOK, LANES), 1)
    chosen = onehot((lane == r0) | (lane == r1_))
    lower = onehot(iota((TOK, TOK), 1) < iota((TOK, TOK), 0))
    earlier = mm(lower, chosen)
    p0 = jnp.sum(jnp.where(lane == r0, earlier, 0.0), axis=1, keepdims=True).astype(jnp.int32)
    p1 = jnp.sum(jnp.where(lane == r1_, earlier, 0.0), axis=1, keepdims=True).astype(jnp.int32)
    slot = iota((TOK, GROUPS * PAD), 1)
    m0 = onehot(slot == r0 * PAD + p0)
    m1 = onehot(slot == r1_ * PAD + p1)
    emb_lo = onehot(iota((TOK, LANES), 1) == iota((TOK, LANES), 0))
    emb_hi = onehot(iota((TOK, LANES), 1) == iota((TOK, LANES), 0) + HIGH)
    tok_e = mm(tok[...], emb_lo)
    cot_e = mm(cot[...], emb_hi)
    a0 = (tok_e + w0 * cot_e).astype(BF)
    a1 = (tok_e + w1 * cot_e).astype(BF)
    dsend[...] = (mm_tn(m0, a0) + mm_tn(m1, a1)).astype(BF)

    pl.semaphore_wait(bar, 21)

    mine = pl.ds(pl.multiple_of(e * PAD, PAD), PAD)
    copies = []
    for d in range(1, 8):
        there = pl.ds(pl.multiple_of(((e + d) % GROUPS) * PAD, PAD), PAD)
        copies.append(send(dsend.at[there], drecv.at[mine], dss.at[d], drs.at[d], at_e(d)))
    drecv[mine, :] = dsend[mine, :]
    l_ = iota((LANES, WIDE), 0)
    c_ = iota((LANES, WIDE), 1)
    for k in range(SIDE):
        plo[pl.ds(k * LANES, LANES), :] = onehot((c_ - l_ == TOK * k) & (l_ < TOK))
        phi[pl.ds(k * LANES, LANES), :] = onehot((c_ - l_ == TOK * k - HIGH) & (l_ >= HIGH) & (l_ < HIGH + TOK))
    q_ = iota((ROWS, GROUPS * PAD), 1)
    s_ = iota((ROWS, GROUPS * PAD), 0)
    compact = onehot((s_ == (q_ >> 5) * CAP + (q_ & 31)) & ((q_ & 31) < CAP))
    for c in copies:
        c.wait()

    rows = mm(compact, drecv[...])
    lo, hi = rows[:HALF], rows[HALF:]
    low_lane = iota((HALF, LANES), 1) < HIGH
    t1[y] = jnp.where(low_lane, lo, pltpu.roll(hi, HIGH, 1)).astype(BF)
    g1[z] = jnp.where(low_lane, pltpu.roll(lo, HIGH, 1), hi).astype(BF)

    copies = []
    for d in range(1, 8):
        copies.append(send(t1.at[y], t1.at[y], s1.at[0, d], r1.at[0, d], at_y(d)))
        copies.append(send(g1.at[z], g1.at[z], s1.at[1, d], r1.at[1, d], at_z(d)))
    for c in copies:
        c.wait()

    def unpack(ref):
        flat = jnp.concatenate([ref[k] for k in range(SIDE)], axis=1)
        return jnp.concatenate([mm(flat, plo[...]), mm(flat, phi[...])], axis=0).astype(BF)

    t2[0] = unpack(t1)
    g2[0] = unpack(g1)

    sends = {}
    for d in ORDER:
        sends[d] = (
            send(t2.at[0], t2.at[d], s2.at[0, d], r2.at[0, d], at_z(d)),
            send(g2.at[0], g2.at[d], s2.at[1, d], r2.at[1, d], at_y(d)),
        )
    for c in loads:
        c.wait()

    def wcols(k):
        return pl.ds(pl.multiple_of(k * WIDE, LANES), WIDE)

    def wrows(k):
        return wgu[k].reshape(WIDE, 2 * HID)

    gate_up = mm(t2[0], wrows(z))
    grad_h = mm_nt(g2[0], wdv[:, wcols(y)])
    for d in ORDER:
        sends[d][0].wait()
        gate_up += mm(t2[d], wrows((z + SIDE - d) % SIDE))
        sends[d][1].wait()
        grad_h += mm_nt(g2[d], wdv[:, wcols((y + SIDE - d) % SIDE)])

    gate, up = gate_up[:, :HID], gate_up[:, HID:]
    sig = 1.0 / (1.0 + jnp.exp(-gate))
    swish = gate * sig
    hidden = (swish * up).astype(BF)
    grad_gate = (grad_h * up * sig * (1.0 + gate * (1.0 - sig))).astype(BF)
    grad_up = (grad_h * swish).astype(BF)
    grads = jnp.concatenate([grad_gate, grad_up], axis=1)

    sends = {}
    for d in ORDER:
        ms[d] = mm(hidden, wdv[:, wcols((y + d) % SIDE)]).astype(BF)
        gs[d] = mm_nt(grads, wrows((z + d) % SIDE)).astype(BF)
        sends[d] = (
            send(ms.at[d], mr.at[d], s3.at[0, d], r3.at[0, d], at_y(d)),
            send(gs.at[d], gr.at[d], s3.at[1, d], r3.at[1, d], at_z(d)),
        )
    msum = mm(hidden, wdv[:, wcols(y)])
    gsum = mm_nt(grads, wrows(z))
    for d in ORDER:
        sends[d][0].wait()
        msum += mr[d].astype(F32)
        sends[d][1].wait()
        gsum += gr[d].astype(F32)

    def pack(total):
        r = total.astype(BF)
        return mm_nt(r[:HALF], plo[...]) + mm_nt(r[HALF:], phi[...])

    mall = pack(msum).astype(BF)
    gall = pack(gsum).astype(BF)
    for k in range(SIDE):
        mp[k] = mall[:, k * LANES:(k + 1) * LANES]
        gp[k] = gall[:, k * LANES:(k + 1) * LANES]
    copies = []
    for d in range(1, 8):
        copies.append(send(mp.at[(z + d) % SIDE], mq.at[d], s4.at[0, d], r4.at[0, d], at_z(d)))
        copies.append(send(gp.at[(y + d) % SIDE], gq.at[d], s4.at[1, d], r4.at[1, d], at_y(d)))
    mtot = mp[z].astype(F32)
    gtot = gp[y].astype(F32)
    for c in copies:
        c.wait()
    for d in range(1, 8):
        mtot += mq[d].astype(F32)
        gtot += gq[d].astype(F32)

    lo = jnp.where(low_lane, mtot, pltpu.roll(gtot, HIGH, 1))
    hi = jnp.where(low_lane, pltpu.roll(mtot, HIGH, 1), gtot)
    both = jnp.concatenate([lo, hi], axis=0).astype(BF)
    rsend[...] = mm_tn(compact, both).astype(BF)
    copies = []
    for d in range(1, 8):
        there = pl.ds(pl.multiple_of(((e + d) % GROUPS) * PAD, PAD), PAD)
        copies.append(send(rsend.at[there], rrecv.at[mine], rss.at[d], rrs.at[d], at_e(d)))
    rrecv[mine, :] = rsend[mine, :]
    for c in copies:
        c.wait()
    back = rrecv[...]
    b0 = mm(m0, back)
    b1 = mm(m1, back)
    mixed[...] = (w0 * b0 + w1 * b1)[:, :TOK].astype(BF)
    gin[...] = pltpu.roll(b0 + b1, HIGH, 1)[:, :TOK].astype(BF)


def shards(tokens, cotangent, routes, route_weight, w_gate, w_up, w_down):
    vm = pl.BlockSpec(memory_space=pltpu.VMEM)
    hbm = pl.BlockSpec(memory_space=pl.ANY)
    dma = pltpu.SemaphoreType.DMA
    small = pltpu.VMEM((SIDE, HALF, LANES), BF)
    big = pltpu.VMEM((SIDE, ROWS, WIDE), BF)
    table = pltpu.VMEM((SIDE * LANES, WIDE), BF)
    block = pltpu.VMEM((GROUPS * PAD, LANES), BF)
    out = jax.ShapeDtypeStruct((TOK, TOK), BF)
    return pl.pallas_call(
        kernel,
        out_shape=(out, out),
        in_specs=[vm] * 4 + [hbm] * 3,
        out_specs=(vm, vm),
        scratch_shapes=[
            pltpu.VMEM((SIDE, SIDE, TOK, 2 * HID), BF),
            pltpu.VMEM((HID, SIDE * WIDE), BF),
            table, table, block, block,
            small, small, big, big, big, big, big, big, small, small, small, small, block, block,
            dma((2 * SIDE + 1,)), dma((8,)), dma((8,)),
            dma((2, 8)), dma((2, 8)), dma((2, 8)), dma((2, 8)),
            dma((2, 8)), dma((2, 8)), dma((2, 8)), dma((2, 8)),
            dma((8,)), dma((8,)),
        ],
        compiler_params=pltpu.CompilerParams(
            collective_id=0, has_side_effects=True, vmem_limit_bytes=40 * 2**20
        ),
        name="moe",
    )(
        tokens, cotangent, routes, route_weight,
        w_gate.reshape(SIDE, SIDE, TOK, HID), w_up.reshape(SIDE, SIDE, TOK, HID), w_down[0],
    )


def solution(mesh):
    return jax.shard_map(
        shards,
        mesh=mesh,
        in_specs=(
            P("expert", "tensor"),
            P("expert", "tensor"),
            P("expert", None),
            P("expert", None),
            P("expert", None, "tensor"),
            P("expert", None, "tensor"),
            P("expert", "tensor", None),
        ),
        out_specs=(P("expert", "tensor"), P("expert", "tensor")),
        check_vma=False,
    )
```

time: 651 us -> 99.4 us (0.15)
  waiting for transfers between devices: 497 us -> 0 us
  Pallas kernels: 0 us -> 90.1 us
  blocking collectives: 80 us -> 0 us
  starting transfers between devices: 33.4 us -> 0 us
  between operations: 14.3 us -> 0.64 us
  matrix products: 8.97 us -> 0 us
    reduce_scatter x2 -> x0, waiting for transfers between devices: 492 us -> none  [the longest x1 256 us: shards(): lax.psum_scatter(grad_input, 'tensor', scatter_dimension=1, tiled=True)]
    pallas_call x0 -> x1, Pallas kernels: none -> 90.1 us  [shards(): pl.pallas_call(kernel, out_shape=(out, out), in_specs=[vm] * 4 + [hbm] *...]
    all_gather x2 -> x0, blocking collectives: 80 us -> none  [the longest x1 43.4 us: shards(): piece_tokens = lax.all_gather(recv_tokens, 'tensor', axis=1, tiled=True)]
    all_to_all x4 -> x0, starting transfers between devices: 33.4 us -> none  [the longest x1 10.1 us: shards(): lax.all_to_all(send_tokens, 'expert', split_axis=0, concat_axis=0, tiled=...]
    dot_general x8 -> x0, matrix products: 8.97 us -> none  [the longest x3 3.61 us: contract_last(): lax.dot_general(left, right, (((1,), (1,)), ((), ())), preferred_element_...]
  transfers between devices with their start and end apart: 6 -> 0, of which waited for: 4 -> 0; matrix products, arithmetic and copies ran while one was open for 2% -> 0% of each run, Pallas kernels for 0% -> 0%
where the time goes in v1:
time: 99.4 us; the launch traced here: 99.1 us
  Pallas kernels  90.1 us (91%)
  local copies, waits for them, and re-layouts  8.36 us (8%)
    pallas_call x1, Pallas kernels, shards(): pl.pallas_call(kernel, out_shape=(out, out), in_specs=[vm] * 4 + [hbm] *...  90.1 us
    unnamed x14, local copies, waits for them, and re-layouts  8.36 us

profile of v1, /device:TPU:1, one launch (start us, length us, event | category | flops | bytes accessed | tf_op | source)
XLA Modules:
  0.0 99.1 jit_solution(16123301348006716344)
XLA Ops:
  0.6 0.8 copy.9.routes
  1.4 0.8 copy.10.rw
  2.2 0.0 copy-start
  2.2 1.4 %copy-done = bf16[1,3072,256]{2,1,0:T(8,128)(2,1)S(1)} copy-done((bf16[1,3072,256]{2,1,0:T(8,128)(2,1)S(1)}, bf16[1,3072,256]{2,1,0:T(8,128)(2,1)}, u32[]{:S(2)}) %copy-start) | copy-done | bytes 1572888
  3.6 0.0 copy-start.1
  3.6 1.4 %copy-done.1 = bf16[1,3072,256]{2,1,0:T(8,128)(2,1)S(1)} copy-done((bf16[1,3072,256]{2,1,0:T(8,128)(2,1)S(1)}, bf16[1,3072,256]{2,1,0:T(8,128)(2,1)}, u32[]{:S(2)}) %copy-start.1) | copy-done | bytes 1572888
  5.0 0.0 copy-start.2
  5.0 1.4 %copy-done.2 = bf16[1,256,3072]{2,1,0:T(8,128)(2,1)S(1)} copy-done((bf16[1,256,3072]{2,1,0:T(8,128)(2,1)S(1)}, bf16[1,256,3072]{2,1,0:T(8,128)(2,1)}, u32[]{:S(2)}) %copy-start.2) | copy-done | bytes 1572888
  6.4 0.0 copy-start.3
  6.4 0.7 copy-done.3
  7.1 0.0 copy-start.4
  7.1 0.7 copy-done.4
  7.8 90.1 %moe.1 = (bf16[48,48]{1,0:T(8,128)(2,1)S(1)}, bf16[48,48]{1,0:T(8,128)(2,1)S(1)}) custom-call(bf16[48,48]{1,0:T(8,128)(2,1)S(1)} %copy-done.3, bf16[48,48]{1,0:T(8,128)(2,1)S(1)} %copy-done.4, s32[48,2]{1,0:T(8,128)S(1)} %copy.9.routes, f32[48,2]{1,0:T(8,128)S(1)} %copy.10.rw, bf16[8,8,48,256]{3,2,1,0:T(8,128)(2,1)S(1)} %bitcast.3, ...), custom_call_target="tpu_custom_call" | custom-call | tf_op jit(solution)/shard_map/moe/pallas_call | solution.py:242
  97.9 0.6 copy.13
  98.5 0.6 copy.14
Async XLA Ops:
  2.2 1.4 %copy-start = (bf16[1,3072,256]{2,1,0:T(8,128)(2,1)S(1)}, bf16[1,3072,256]{2,1,0:T(8,128)(2,1)}, u32[]{:S(2)}) copy-start(bf16[1,3072,256]{2,1,0:T(8,128)(2,1)} %param.11) | copy-start | bytes 4718596
  3.6 1.4 %copy-start.1 = (bf16[1,3072,256]{2,1,0:T(8,128)(2,1)S(1)}, bf16[1,3072,256]{2,1,0:T(8,128)(2,1)}, u32[]{:S(2)}) copy-start(bf16[1,3072,256]{2,1,0:T(8,128)(2,1)} %param.12) | copy-start | bytes 4718596
  5.0 1.4 %copy-start.2 = (bf16[1,256,3072]{2,1,0:T(8,128)(2,1)S(1)}, bf16[1,256,3072]{2,1,0:T(8,128)(2,1)}, u32[]{:S(2)}) copy-start(bf16[1,256,3072]{2,1,0:T(8,128)(2,1)} %param.13) | copy-start | bytes 4718596
  6.4 0.7 copy-start.3
  7.1 0.7 copy-start.4

commit v2 on v1

--- a/solution.py
+++ b/solution.py
@@ -22,7 +22,6 @@
 HID = 256
 LANES = 128
 HIGH = 64
-ORDER = (1, 7, 2, 6, 3, 5, 4)
 
 
 def iota(shape, dim):
@@ -46,10 +45,11 @@
 
 
 def kernel(
-    tok, cot, routes, rw, wg, wu, wd,
+    tok_h, cot_h, routes_h, rw_h, wg, wu, wd,
     mixed, gin,
+    tok, cot, routes, rw, isem,
     wgu, wdv, plo, phi, dsend, drecv,
-    t1, g1, t2, g2, ms, gs, mr, gr, mp, gp, mq, gq, rsend, rrecv,
+    t1, g1, t2, g2, pm, pg, ms, gs, mr, gr, mp, gp, mq, gq, rsend, rrecv,
     wsem, dss, drs, s1, r1, s2, r2, s3, r3, s4, r4, rss, rrs,
 ):
     e = lax.axis_index("expert")
@@ -66,6 +66,12 @@
     def at_z(d):
         return (e, y * SIDE + (z + d) % SIDE)
 
+    first = [
+        pltpu.make_async_copy(a, b, isem.at[k])
+        for k, (a, b) in enumerate(((routes_h, routes), (tok_h, tok), (cot_h, cot), (rw_h, rw)))
+    ]
+    for c in first:
+        c.start()
     loads = []
     for k in range(SIDE):
         loads.append(pltpu.make_async_copy(wg.at[:, k], wgu.at[k, :, :, pl.ds(0, HID)], wsem.at[k]))
@@ -86,8 +92,16 @@
         c.start()
         return c
 
-    r0, r1_ = routes[:, 0:1], routes[:, 1:2]
-    w0, w1 = rw[:, 0:1], rw[:, 1:2]
+    for c in first:
+        c.wait()
+    eye = iota((TOK, TOK), 0) == iota((TOK, TOK), 1)
+
+    def column(row):
+        return jnp.sum(jnp.where(eye, row, 0.0), axis=1, keepdims=True)
+
+    ids = routes[...].astype(F32)
+    r0, r1_ = column(ids[0:1]).astype(jnp.int32), column(ids[1:2]).astype(jnp.int32)
+    w0, w1 = column(rw[0:1, :]), column(rw[1:2, :])
     lane = iota((TOK, LANES), 1)
     chosen = onehot((lane == r0) | (lane == r1_))
     lower = onehot(iota((TOK, TOK), 1) < iota((TOK, TOK), 0))
@@ -144,12 +158,22 @@
     t2[0] = unpack(t1)
     g2[0] = unpack(g1)
 
-    sends = {}
-    for d in ORDER:
-        sends[d] = (
-            send(t2.at[0], t2.at[d], s2.at[0, d], r2.at[0, d], at_z(d)),
-            send(g2.at[0], g2.at[d], s2.at[1, d], r2.at[1, d], at_y(d)),
+    up_ring = ((1, 0), (1, 1), (2, 0), (2, 1), (3, 0), (3, 1), (4, 0))
+    down_ring = ((7, 1), (7, 0), (6, 1), (6, 0), (5, 1), (5, 0), (4, 1))
+
+    def half(h):
+        return pl.ds(h * HALF, HALF)
+
+    def hop(buf, way, n, at, a):
+        k, h = (up_ring, down_ring)[way][n]
+        before = (k - 1) if way == 0 else (k + 1) % SIDE
+        return send(
+            buf.at[before, half(h)], buf.at[k, half(h)],
+            s2.at[a, way, n], r2.at[a, way, n], at(1 if way == 0 else SIDE - 1),
         )
+
+    streams = [(t2, 0, at_z, 0), (t2, 1, at_z, 0), (g2, 0, at_y, 1), (g2, 1, at_y, 1)]
+    hops = [[hop(buf, way, n, at, a) for n in range(2)] for buf, way, at, a in streams]
     for c in loads:
         c.wait()
 
@@ -161,11 +185,19 @@
 
     gate_up = mm(t2[0], wrows(z))
     grad_h = mm_nt(g2[0], wdv[:, wcols(y)])
-    for d in ORDER:
-        sends[d][0].wait()
-        gate_up += mm(t2[d], wrows((z + SIDE - d) % SIDE))
-        sends[d][1].wait()
-        grad_h += mm_nt(g2[d], wdv[:, wcols((y + SIDE - d) % SIDE)])
+    for n in range(7):
+        for c, (buf, way, at, a) in zip(hops, streams):
+            c[n].wait_recv()
+            if n + 2 < 7:
+                c.append(hop(buf, way, n + 2, at, a))
+        if n % 2 == 1 or n == 6:
+            k = n // 2 + 1
+            for d in (k, SIDE - k) if k < 4 else (4,):
+                gate_up += mm(t2[d], wrows((z + SIDE - d) % SIDE))
+                grad_h += mm_nt(g2[d], wdv[:, wcols((y + SIDE - d) % SIDE)])
+    for c in hops:
+        for x in c:
+            x.wait_send()
 
     gate, up = gate_up[:, :HID], gate_up[:, HID:]
     sig = 1.0 / (1.0 + jnp.exp(-gate))
@@ -175,21 +207,58 @@
     grad_up = (grad_h * swish).astype(BF)
     grads = jnp.concatenate([grad_gate, grad_up], axis=1)
 
-    sends = {}
-    for d in ORDER:
-        ms[d] = mm(hidden, wdv[:, wcols((y + d) % SIDE)]).astype(BF)
-        gs[d] = mm_nt(grads, wrows((z + d) % SIDE)).astype(BF)
-        sends[d] = (
-            send(ms.at[d], mr.at[d], s3.at[0, d], r3.at[0, d], at_y(d)),
-            send(gs.at[d], gr.at[d], s3.at[1, d], r3.at[1, d], at_z(d)),
-        )
-    msum = mm(hidden, wdv[:, wcols(y)])
-    gsum = mm_nt(grads, wrows(z))
-    for d in ORDER:
-        sends[d][0].wait()
-        msum += mr[d].astype(F32)
-        sends[d][1].wait()
-        gsum += gr[d].astype(F32)
+    up_sum = ((4, 0), (3, 1), (3, 0), (2, 1), (2, 0), (1, 1), (1, 0))
+    down_sum = ((4, 1), (5, 0), (5, 1), (6, 0), (6, 1), (7, 0), (7, 1))
+
+    def partial(d):
+        pm[d] = mm(hidden, wdv[:, wcols((y + d) % SIDE)])
+        pg[d] = mm_nt(grads, wrows((z + d) % SIDE))
+
+    streams = [(pm, ms, mr, 0, at_y, 0), (pm, ms, mr, 1, at_y, 0), (pg, gs, gr, 0, at_z, 1), (pg, gs, gr, 1, at_z, 1)]
+    hops = [[] for _ in streams]
+
+    def pass_on(n):
+        for c, (part, sbuf, rbuf, way, at, a) in zip(hops, streams):
+            d, h = (up_sum, down_sum)[way][n]
+            value = part[d, half(h), :]
+            if n >= 2:
+                c[n - 2].wait_recv()
+                value += rbuf[way, n - 2].astype(F32)
+            sbuf[way, n] = value.astype(BF)
+            c.append(send(
+                sbuf.at[way, n], rbuf.at[way, n],
+                s3.at[a, way, n], r3.at[a, way, n], at(1 if way == 0 else SIDE - 1),
+            ))
+
+    partial(4)
+    pass_on(0)
+    partial(3)
+    partial(5)
+    pass_on(1)
+    partial(2)
+    partial(6)
+    pass_on(2)
+    pass_on(3)
+    partial(1)
+    partial(7)
+    pass_on(4)
+    pass_on(5)
+    partial(0)
+    pass_on(6)
+    sums = []
+    for i, (part, rbuf) in enumerate(((pm, mr), (pg, gr))):
+        one, two = hops[2 * i], hops[2 * i + 1]
+        halves = [None, None]
+        for n in (5, 6):
+            one[n].wait_recv()
+            two[n].wait_recv()
+        halves[0] = part[0, half(0), :] + rbuf[0, 6].astype(F32) + rbuf[1, 5].astype(F32)
+        halves[1] = part[0, half(1), :] + rbuf[0, 5].astype(F32) + rbuf[1, 6].astype(F32)
+        sums.append(jnp.concatenate(halves, axis=0))
+    msum, gsum = sums
+    for c in hops:
+        for x in c:
+            x.wait_send()
 
     def pack(total):
         r = total.astype(BF)
@@ -238,28 +307,32 @@
     big = pltpu.VMEM((SIDE, ROWS, WIDE), BF)
     table = pltpu.VMEM((SIDE * LANES, WIDE), BF)
     block = pltpu.VMEM((GROUPS * PAD, LANES), BF)
+    tall = pltpu.VMEM((SIDE, ROWS, WIDE), F32)
+    sums = pltpu.VMEM((2, 7, HALF, WIDE), BF)
     out = jax.ShapeDtypeStruct((TOK, TOK), BF)
     return pl.pallas_call(
         kernel,
         out_shape=(out, out),
-        in_specs=[vm] * 4 + [hbm] * 3,
+        in_specs=[hbm] * 7,
         out_specs=(vm, vm),
         scratch_shapes=[
+            pltpu.VMEM((TOK, TOK), BF), pltpu.VMEM((TOK, TOK), BF),
+            pltpu.VMEM((2, TOK), jnp.int32), pltpu.VMEM((2, TOK), F32), dma((4,)),
             pltpu.VMEM((SIDE, SIDE, TOK, 2 * HID), BF),
             pltpu.VMEM((HID, SIDE * WIDE), BF),
             table, table, block, block,
-            small, small, big, big, big, big, big, big, small, small, small, small, block, block,
+            small, small, big, big, tall, tall, sums, sums, sums, sums, small, small, small, small, block, block,
             dma((2 * SIDE + 1,)), dma((8,)), dma((8,)),
-            dma((2, 8)), dma((2, 8)), dma((2, 8)), dma((2, 8)),
-            dma((2, 8)), dma((2, 8)), dma((2, 8)), dma((2, 8)),
+            dma((2, 8)), dma((2, 8)), dma((2, 2, 7)), dma((2, 2, 7)),
+            dma((2, 2, 7)), dma((2, 2, 7)), dma((2, 8)), dma((2, 8)),
             dma((8,)), dma((8,)),
         ],
         compiler_params=pltpu.CompilerParams(
-            collective_id=0, has_side_effects=True, vmem_limit_bytes=40 * 2**20
+            collective_id=0, has_side_effects=True, vmem_limit_bytes=60 * 2**20
         ),
         name="moe",
     )(
-        tokens, cotangent, routes, route_weight,
+        tokens, cotangent, routes.T, route_weight.T,
         w_gate.reshape(SIDE, SIDE, TOK, HID), w_up.reshape(SIDE, SIDE, TOK, HID), w_down[0],
     )
 

time: 99.4 us -> 76.5 us (0.77)
  Pallas kernels: 90.1 us -> 73 us
  local copies, waits for them, and re-layouts: 8.36 us -> 2.61 us
    pallas_call x1, Pallas kernels: 90.1 us -> 73 us  [shards(): pl.pallas_call(kernel, out_shape=(out, out), in_specs=[hbm] * 7, out_spec...]
    unnamed x14 -> x2, local copies, waits for them, and re-layouts: 8.36 us -> 2.61 us
where the time goes in v2:
time: 76.5 us; the launch traced here: 76.2 us
  Pallas kernels  73 us (95%)
  local copies, waits for them, and re-layouts  2.61 us (3%)
    pallas_call x1, Pallas kernels, shards(): pl.pallas_call(kernel, out_shape=(out, out), in_specs=[hbm] * 7, out_spec...  73 us
    unnamed x2, local copies, waits for them, and re-layouts  2.61 us

profile of v2, /device:TPU:1, one launch (start us, length us, event | category | flops | bytes accessed | tf_op | source)
XLA Modules:
  0.0 76.2 jit_solution(5887207837666319357)
XLA Ops:
  0.6 73.0 %moe.1 = (bf16[48,48]{1,0:T(8,128)(2,1)}, bf16[48,48]{1,0:T(8,128)(2,1)}) custom-call(bf16[48,48]{1,0:T(8,128)(2,1)} %tok_h.1, bf16[48,48]{1,0:T(8,128)(2,1)} %cot_h.1, s32[2,48]{1,0:T(2,128)} %bitcast.8, f32[2,48]{1,0:T(2,128)} %bitcast.9, bf16[8,8,48,256]{3,2,1,0:T(8,128)(2,1)} %bitcast.5, bf16[8,8,48,256]{3,2,1,0:T(8,128)(2,1)} %bitcast.6, ...), custom_call_target="tpu_custom_call" | custom-call | tf_op jit(solution)/shard_map/moe/pallas_call | solution.py:313
  73.6 1.3 %copy.11 = bf16[48,48]{1,0:T(8,128)(2,1)} copy(bf16[48,48]{1,0:T(8,128)(2,1)} %get-tuple-element.4) | data formatting | bytes 9216
  74.9 1.3 %copy.12 = bf16[48,48]{1,0:T(8,128)(2,1)} copy(bf16[48,48]{1,0:T(8,128)(2,1)} %get-tuple-element.5) | data formatting | bytes 9216

commit v3 on v1

v3 whole, which is shorter than its diff:
```python
import jax
import jax.numpy as jnp
from jax import lax
from jax.experimental import pallas as pl
from jax.experimental.pallas import tpu as pltpu
from jax.sharding import PartitionSpec as P

MESH = pl.DeviceIdType.MESH
BF = jnp.bfloat16
F32 = jnp.float32

GROUPS = 8
SIDE = 8
TOK = 48
CAP = 20
PAD = 48
ROWS = GROUPS * CAP
HALF = ROWS // 2
WIDE = SIDE * TOK
HID = 256
LANES = 128
FAR = (4, 3, 5, 2, 6, 1, 7)
NEAR = (0, 1, 7, 2, 6, 3, 5, 4)


def iota(shape, dim):
    return lax.broadcasted_iota(jnp.int32, shape, dim)


def onehot(cond):
    return jnp.where(cond, 1.0, 0.0).astype(BF)


def mm(a, b):
    return lax.dot_general(a, b, (((1,), (0,)), ((), ())), preferred_element_type=F32)


def mm_tn(a, b):
    return lax.dot_general(a, b, (((0,), (0,)), ((), ())), preferred_element_type=F32)


def mm_nt(a, b):
    return lax.dot_general(a, b, (((1,), (1,)), ((), ())), preferred_element_type=F32)


def half(h):
    return pl.ds(h * HALF, HALF)


def kernel(
    tok_h, cot_h, routes_h, rw_h, wg, wu, wd,
    mixed, gin,
    tok, cot, routes, rw, isem,
    wgu, wdv, spread, comp, dsend, drecv, rsend, rrecv,
    t1, g1, t2, g2, pm, pg, ms, gs, mr, gr, mp, gp, mq, gq,
    wsem, s1, r1, ds_, dr, s2, r2, s3, r3, rs_, rr, s4, r4,
):
    e = lax.axis_index("expert")
    t = lax.axis_index("tensor")
    y = t // SIDE
    z = t % SIDE

    def at_e(d):
        return ((e + d + GROUPS) % GROUPS, t)

    def at_y(d):
        return (e, ((y + d + SIDE) % SIDE) * SIDE + z)

    def at_z(d):
        return (e, y * SIDE + (z + d + SIDE) % SIDE)

    def send(src, dst, ss, rs, where):
        c = pltpu.make_async_remote_copy(
            src_ref=src, dst_ref=dst, send_sem=ss, recv_sem=rs, device_id=where, device_id_type=MESH
        )
        c.start()
        return c

    first = [
        pltpu.make_async_copy(a, b, isem.at[k])
        for k, (a, b) in enumerate(((tok_h, tok), (cot_h, cot), (routes_h, routes), (rw_h, rw)))
    ]
    for c in first:
        c.start()
    bar = pltpu.get_barrier_semaphore()
    for at in (at_y, at_z, at_e):
        for d in FAR:
            pl.semaphore_signal(bar, inc=1, device_id=at(d), device_id_type=MESH)
    loads = []
    for k in range(SIDE):
        loads.append(pltpu.make_async_copy(wg.at[:, k], wgu.at[k, :, :, pl.ds(0, HID)], wsem.at[k]))
        loads.append(pltpu.make_async_copy(wu.at[:, k], wgu.at[k, :, :, pl.ds(HID, HID)], wsem.at[SIDE + k]))
    loads.append(pltpu.make_async_copy(wd, wdv, wsem.at[2 * SIDE]))

    zero = jnp.zeros((TOK, LANES), BF)
    t1[y] = zero
    g1[z] = zero
    first[0].wait()
    first[1].wait()
    t1[y, :, :TOK] = tok[...]
    g1[z, :, :TOK] = cot[...]
    pl.semaphore_wait(bar, 21)

    copies = []
    for d in FAR:
        copies.append(send(t1.at[y], t1.at[y], s1.at[0, d], r1.at[0, d], at_y(d)))
        copies.append(send(g1.at[z], g1.at[z], s1.at[1, d], r1.at[1, d], at_z(d)))
    for c in loads:
        c.start()

    first[2].wait()
    first[3].wait()
    eye = iota((TOK, TOK), 0) == iota((TOK, TOK), 1)

    def column(row):
        return jnp.sum(jnp.where(eye, row, 0.0), axis=1, keepdims=True)

    ids = routes[...].astype(F32)
    e0, e1 = column(ids[0:1]).astype(jnp.int32), column(ids[1:2]).astype(jnp.int32)
    w0, w1 = column(rw[0:1, :]), column(rw[1:2, :])
    lane = iota((TOK, LANES), 1)
    chosen = onehot((lane == e0) | (lane == e1))
    lower = onehot(iota((TOK, TOK), 1) < iota((TOK, TOK), 0))
    earlier = mm(lower, chosen)
    p0 = jnp.sum(jnp.where(lane == e0, earlier, 0.0), axis=1, keepdims=True).astype(jnp.int32) + e0 * PAD
    p1 = jnp.sum(jnp.where(lane == e1, earlier, 0.0), axis=1, keepdims=True).astype(jnp.int32) + e1 * PAD
    slot = iota((TOK, GROUPS * PAD), 1)
    m0 = onehot(slot == p0)
    m1 = onehot(slot == p1)
    n0 = onehot(slot == p0 + CAP)
    n1 = onehot(slot == p1 + CAP)
    l_ = iota((LANES, WIDE), 0)
    c_ = iota((LANES, WIDE), 1)
    for k in range(SIDE):
        spread[pl.ds(k * LANES, LANES), :] = onehot((c_ - l_ == TOK * k) & (l_ < TOK))
    q_ = iota((HALF, GROUPS // 2 * PAD), 1)
    s_ = iota((HALF, GROUPS // 2 * PAD), 0)
    group = ((q_.astype(F32) + 0.5) * (1.0 / PAD)).astype(jnp.int32)
    place = q_ - group * PAD
    row = group * CAP + place
    comp[pl.ds(0, HALF), :] = onehot((row == s_) & (place < CAP))
    comp[pl.ds(HALF, HALF), :] = onehot((row == s_ + CAP) & (place >= CAP) & (place < 2 * CAP))
    for c in copies:
        c.wait()

    def unpack(ref):
        return mm(jnp.concatenate([ref[k] for k in range(SIDE)], axis=1), spread[...])

    tu = unpack(t1).astype(BF)
    gu = unpack(g1)
    left = jnp.concatenate([m0 + m1, n0, n1], axis=0)
    right = jnp.concatenate([tu, (w0 * gu).astype(BF), (w1 * gu).astype(BF)], axis=0)
    dsend[...] = mm_tn(left, right).astype(BF)
    mine = pl.ds(pl.multiple_of(e * PAD, PAD), PAD)

    def there(d):
        return pl.ds(pl.multiple_of(((e + d) % GROUPS) * PAD, PAD), PAD)

    def place_of(d):
        return pl.ds(NEAR.index(d) * PAD, PAD)

    copies = {}
    for o in NEAR[1:]:
        d = GROUPS - o
        copies[o] = send(dsend.at[there(d)], drecv.at[place_of(o)], ds_.at[d], dr.at[d], at_e(d))
    drecv[place_of(0), :] = dsend[mine, :]

    def arrive(b):
        for o in NEAR[4 * b : 4 * b + 4]:
            if o:
                copies[o].wait_recv()
        rows = mm(comp[...], drecv[pl.ds(b * 4 * PAD, 4 * PAD), :]).astype(BF)
        t2[0, half(b), :] = rows[:HALF]
        g2[0, half(b), :] = rows[HALF:]

    pairs = ((t2, at_z, 0), (g2, at_y, 1))
    moves = {}

    def go(b, n, src, dst, dist):
        for buf, at, a in pairs:
            moves[a, b, n] = send(
                buf.at[src, half(b)], buf.at[dst, half(b)], s2.at[a, b, n], r2.at[a, b, n], at(dist)
            )

    def arrived(b, *ns):
        for n in ns:
            for a in range(2):
                moves[a, b, n].wait_recv()

    def wcols(k):
        return pl.ds(pl.multiple_of(k * WIDE, LANES), WIDE)

    def wrows(k):
        return wgu[k].reshape(WIDE, 2 * HID)

    acc = [[0.0, 0.0], [0.0, 0.0]]

    def use(b, *ds):
        for d in ds:
            acc[b][0] += mm(t2[d, half(b), :], wrows((z + SIDE - d) % SIDE))
            acc[b][1] += mm_nt(g2[d, half(b), :], wdv[:, wcols((y + SIDE - d) % SIDE)])

    def two(b):
        go(b, 0, 0, 2, 2)
        go(b, 1, 0, 6, -2)

    def one(b):
        go(b, 2, 0, 1, 1)
        go(b, 3, 0, 7, -1)

    def pass_on(b):
        for n in (b, 1 - b):
            arrived(b, n)
            src, step = (2, 1) if n == 0 else (6, -1)
            if n == b:
                go(b, 6, src, 4, 2 * step)
            go(b, 4 + n, src, src + step, step)

    state = [None, None]

    def activate(b):
        gate, up = acc[b][0][:, :HID], acc[b][0][:, HID:]
        grad_h = acc[b][1]
        sig = 1.0 / (1.0 + jnp.exp(-gate))
        swish = gate * sig
        hidden = (swish * up).astype(BF)
        grad_gate = (grad_h * up * sig * (1.0 + gate * (1.0 - sig))).astype(BF)
        grad_up = (grad_h * swish).astype(BF)
        state[b] = (hidden, jnp.concatenate([grad_gate, grad_up], axis=1))

    sums = ((ms, mr, at_y, 0), (gs, gr, at_z, 1))
    hops = {}

    def term(b, d):
        hidden, grads = state[b]
        return mm(hidden, wdv[:, wcols((y + d) % SIDE)]), mm_nt(grads, wrows((z + d) % SIDE))

    def give(b, n, values, dist):
        for (sbuf, rbuf, at, a), value in zip(sums, values):
            sbuf[b, n] = value.astype(BF)
            hops[a, b, n] = send(sbuf.at[b, n], rbuf.at[b, n], s3.at[a, b, n], r3.at[a, b, n], at(dist))

    def taken(b, n):
        values = []
        for _, rbuf, _, a in sums:
            hops[a, b, n].wait_recv()
            values.append(rbuf[b, n].astype(F32))
        return values

    def add(*terms):
        return [sum(vs[1:], vs[0]) for vs in zip(*terms)]

    def start_sums(b):
        give(b, 0, term(b, 4), 2 if b == 0 else -2)
        give(b, 1, term(b, 3), 1)
        give(b, 2, term(b, 5), -1)
        give(b, 3, term(b, 1), 1)
        give(b, 4, term(b, 7), -1)
        for i, d in enumerate((2, 6)):
            pm[b, i], pg[b, i] = term(b, d)

    def kept(b, d):
        return [pm[b, (d - 2) // 4], pg[b, (d - 2) // 4]]

    def middle_sums(b):
        for way in (1 - b, b):
            d, n = ((2, 1), (6, 2))[way]
            parts = [kept(b, d), taken(b, n)]
            if way == b:
                parts.append(taken(b, 0))
            give(b, 5 + way, add(*parts), 2 if way == 0 else -2)

    backs = []

    def end_sums(b):
        total = add(term(b, 0), taken(b, 3), taken(b, 4), taken(b, 5), taken(b, 6))
        both = jnp.concatenate([v.astype(BF) for v in total], axis=0)
        rsend[pl.ds(b * 4 * PAD, 4 * PAD), :] = mm_tn(comp[...], both).astype(BF)
        for o in NEAR[4 * b : 4 * b + 4]:
            if o:
                backs.append(send(rsend.at[place_of(o)], rrecv.at[mine], rs_.at[o], rr.at[o], at_e(o)))
            else:
                rrecv[mine, :] = rsend[place_of(0), :]

    arrive(0)
    two(0)
    one(0)
    arrive(1)
    two(1)
    for c in loads:
        c.wait()
    use(0, 0)
    pass_on(0)
    one(1)
    use(0, 2, 6)
    arrived(0, 2, 3)
    use(0, 1, 7)
    pass_on(1)
    arrived(0, 4, 5, 6)
    use(0, 3, 5, 4)
    activate(0)
    start_sums(0)
    use(1, 0, 2, 6)
    arrived(1, 2, 3)
    use(1, 1, 7)
    middle_sums(0)
    arrived(1, 4, 5, 6)
    use(1, 3, 5, 4)
    activate(1)
    start_sums(1)
    end_sums(0)
    middle_sums(1)
    end_sums(1)
    for c in backs:
        c.wait()
    back = rrecv[...]
    out = (w0 * mm(m0, back) + w1 * mm(m1, back)).astype(BF)
    grad = mm(n0 + n1, back).astype(BF)

    mall = mm_nt(out, spread[...]).astype(BF)
    gall = mm_nt(grad, spread[...]).astype(BF)
    for k in range(SIDE):
        mp[k] = mall[:, k * LANES:(k + 1) * LANES]
        gp[k] = gall[:, k * LANES:(k + 1) * LANES]
    last = []
    for d in FAR:
        last.append(send(mp.at[(z + d) % SIDE], mq.at[d], s4.at[0, d], r4.at[0, d], at_z(d)))
        last.append(send(gp.at[(y + d) % SIDE], gq.at[d], s4.at[1, d], r4.at[1, d], at_y(d)))
    mtot = mp[z].astype(F32)
    gtot = gp[y].astype(F32)
    for c in last:
        c.wait()
    for d in range(1, 8):
        mtot += mq[d].astype(F32)
        gtot += gq[d].astype(F32)
    mixed[...] = mtot[:, :TOK].astype(BF)
    gin[...] = gtot[:, :TOK].astype(BF)

    for c in (*copies.values(), *moves.values(), *hops.values()):
        c.wait_send()


def shards(tokens, cotangent, routes, route_weight, w_gate, w_up, w_down):
    vm = pl.BlockSpec(memory_space=pltpu.VMEM)
    hbm = pl.BlockSpec(memory_space=pl.ANY)
    dma = pltpu.SemaphoreType.DMA
    small = pltpu.VMEM((SIDE, TOK, LANES), BF)
    big = pltpu.VMEM((SIDE, ROWS, WIDE), BF)
    tall = pltpu.VMEM((2, 2, HALF, WIDE), F32)
    halves = pltpu.VMEM((2, 7, HALF, WIDE), BF)
    block = pltpu.VMEM((GROUPS * PAD, WIDE), BF)
    out = jax.ShapeDtypeStruct((TOK, TOK), BF)
    return pl.pallas_call(
        kernel,
        out_shape=(out, out),
        in_specs=[hbm] * 7,
        out_specs=(vm, vm),
        scratch_shapes=[
            pltpu.VMEM((TOK, TOK), BF), pltpu.VMEM((TOK, TOK), BF),
            pltpu.VMEM((2, TOK), jnp.int32), pltpu.VMEM((2, TOK), F32), dma((4,)),
            pltpu.VMEM((SIDE, SIDE, TOK, 2 * HID), BF),
            pltpu.VMEM((HID, SIDE * WIDE), BF),
            pltpu.VMEM((SIDE * LANES, WIDE), BF),
            pltpu.VMEM((ROWS, GROUPS // 2 * PAD), BF),
            block, block, block, block,
            small, small, big, big, tall, tall,
            halves, halves, halves, halves,
            small, small, small, small,
            dma((2 * SIDE + 1,)), dma((2, 8)), dma((2, 8)), dma((8,)), dma((8,)),
            dma((2, 2, 7)), dma((2, 2, 7)), dma((2, 2, 7)), dma((2, 2, 7)),
            dma((8,)), dma((8,)), dma((2, 8)), dma((2, 8)),
        ],
        compiler_params=pltpu.CompilerParams(
            collective_id=0, has_side_effects=True, vmem_limit_bytes=60 * 2**20
        ),
        name="moe",
    )(
        tokens, cotangent, routes.T, route_weight.T,
        w_gate.reshape(SIDE, SIDE, TOK, HID), w_up.reshape(SIDE, SIDE, TOK, HID), w_down[0],
    )


def solution(mesh):
    return jax.shard_map(
        shards,
        mesh=mesh,
        in_specs=(
            P("expert", "tensor"),
            P("expert", "tensor"),
            P("expert", None),
            P("expert", None),
            P("expert", None, "tensor"),
            P("expert", None, "tensor"),
            P("expert", "tensor", None),
        ),
        out_specs=(P("expert", "tensor"), P("expert", "tensor")),
        check_vma=False,
    )
```

time: 99.4 us -> 73.1 us (0.74)
  Pallas kernels: 90.1 us -> 69.6 us
  local copies, waits for them, and re-layouts: 8.36 us -> 2.61 us
    pallas_call x1, Pallas kernels: 90.1 us -> 69.6 us  [shards(): pl.pallas_call(kernel, out_shape=(out, out), in_specs=[hbm] * 7, out_spec...]
    unnamed x14 -> x2, local copies, waits for them, and re-layouts: 8.36 us -> 2.61 us
where the time goes in v3:
time: 73.1 us; the launch traced here: 72.8 us
  Pallas kernels  69.6 us (95%)
  local copies, waits for them, and re-layouts  2.61 us (4%)
    pallas_call x1, Pallas kernels, shards(): pl.pallas_call(kernel, out_shape=(out, out), in_specs=[hbm] * 7, out_spec...  69.6 us
    unnamed x2, local copies, waits for them, and re-layouts  2.61 us

profile of v3, /device:TPU:1, one launch (start us, length us, event | category | flops | bytes accessed | tf_op | source)
XLA Modules:
  0.0 72.8 jit_solution(7892708217219345371)
XLA Ops:
  0.6 69.6 %moe.1 = (bf16[48,48]{1,0:T(8,128)(2,1)}, bf16[48,48]{1,0:T(8,128)(2,1)}) custom-call(bf16[48,48]{1,0:T(8,128)(2,1)} %tok_h.1, bf16[48,48]{1,0:T(8,128)(2,1)} %cot_h.1, s32[2,48]{1,0:T(2,128)} %bitcast.8, f32[2,48]{1,0:T(2,128)} %bitcast.9, bf16[8,8,48,256]{3,2,1,0:T(8,128)(2,1)} %bitcast.5, bf16[8,8,48,256]{3,2,1,0:T(8,128)(2,1)} %bitcast.6, ...), custom_call_target="tpu_custom_call" | custom-call | tf_op jit(solution)/shard_map/moe/pallas_call | solution.py:353
  70.2 1.3 %copy.11 = bf16[48,48]{1,0:T(8,128)(2,1)} copy(bf16[48,48]{1,0:T(8,128)(2,1)} %get-tuple-element.4) | data formatting | bytes 9216
  71.5 1.3 %copy.12 = bf16[48,48]{1,0:T(8,128)(2,1)} copy(bf16[48,48]{1,0:T(8,128)(2,1)} %get-tuple-element.5) | data formatting | bytes 9216

commit v4 on v3

--- a/solution.py
+++ b/solution.py
@@ -49,7 +49,7 @@
 
 def kernel(
     tok_h, cot_h, routes_h, rw_h, wg, wu, wd,
-    mixed, gin,
+    out_ref,
     tok, cot, routes, rw, isem,
     wgu, wdv, spread, comp, dsend, drecv, rsend, rrecv,
     t1, g1, t2, g2, pm, pg, ms, gs, mr, gr, mp, gp, mq, gq,
@@ -140,14 +140,16 @@
     row = group * CAP + place
     comp[pl.ds(0, HALF), :] = onehot((row == s_) & (place < CAP))
     comp[pl.ds(HALF, HALF), :] = onehot((row == s_ + CAP) & (place >= CAP) & (place < 2 * CAP))
-    for c in copies:
-        c.wait()
-
     def unpack(ref):
         return mm(jnp.concatenate([ref[k] for k in range(SIDE)], axis=1), spread[...])
 
+    for c in copies[0::2]:
+        c.wait_recv()
     tu = unpack(t1).astype(BF)
+    for c in copies[1::2]:
+        c.wait_recv()
     gu = unpack(g1)
+    sent = copies
     left = jnp.concatenate([m0 + m1, n0, n1], axis=0)
     right = jnp.concatenate([tu, (w0 * gu).astype(BF), (w1 * gu).astype(BF)], axis=0)
     dsend[...] = mm_tn(left, right).astype(BF)
@@ -164,6 +166,8 @@
         d = GROUPS - o
         copies[o] = send(dsend.at[there(d)], drecv.at[place_of(o)], ds_.at[d], dr.at[d], at_e(d))
     drecv[place_of(0), :] = dsend[mine, :]
+    for c in sent:
+        c.wait_send()
 
     def arrive(b):
         for o in NEAR[4 * b : 4 * b + 4]:
@@ -311,33 +315,32 @@
     end_sums(0)
     middle_sums(1)
     end_sums(1)
+    for c in (*copies.values(), *moves.values(), *hops.values()):
+        c.wait_send()
     for c in backs:
-        c.wait()
+        c.wait_recv()
     back = rrecv[...]
-    out = (w0 * mm(m0, back) + w1 * mm(m1, back)).astype(BF)
-    grad = mm(n0 + n1, back).astype(BF)
-
-    mall = mm_nt(out, spread[...]).astype(BF)
-    gall = mm_nt(grad, spread[...]).astype(BF)
-    for k in range(SIDE):
-        mp[k] = mall[:, k * LANES:(k + 1) * LANES]
-        gp[k] = gall[:, k * LANES:(k + 1) * LANES]
-    last = []
-    for d in FAR:
-        last.append(send(mp.at[(z + d) % SIDE], mq.at[d], s4.at[0, d], r4.at[0, d], at_z(d)))
-        last.append(send(gp.at[(y + d) % SIDE], gq.at[d], s4.at[1, d], r4.at[1, d], at_y(d)))
+
+    def spread_out(values, buf):
+        flat = mm_nt(values, spread[...]).astype(BF)
+        for k in range(SIDE):
+            buf[k] = flat[:, k * LANES:(k + 1) * LANES]
+
+    spread_out((w0 * mm(m0, back) + w1 * mm(m1, back)).astype(BF), mp)
+    last = [send(mp.at[(z + d) % SIDE], mq.at[d], s4.at[0, d], r4.at[0, d], at_z(d)) for d in FAR]
+    spread_out(mm(n0 + n1, back).astype(BF), gp)
+    last += [send(gp.at[(y + d) % SIDE], gq.at[d], s4.at[1, d], r4.at[1, d], at_y(d)) for d in FAR]
     mtot = mp[z].astype(F32)
     gtot = gp[y].astype(F32)
+    for c in (*backs, *last):
+        c.wait_send()
     for c in last:
-        c.wait()
+        c.wait_recv()
     for d in range(1, 8):
         mtot += mq[d].astype(F32)
         gtot += gq[d].astype(F32)
-    mixed[...] = mtot[:, :TOK].astype(BF)
-    gin[...] = gtot[:, :TOK].astype(BF)
-
-    for c in (*copies.values(), *moves.values(), *hops.values()):
-        c.wait_send()
+    out_ref[0] = mtot[:, :TOK].astype(BF)
+    out_ref[1] = gtot[:, :TOK].astype(BF)
 
 
 def shards(tokens, cotangent, routes, route_weight, w_gate, w_up, w_down):
@@ -349,12 +352,11 @@
     tall = pltpu.VMEM((2, 2, HALF, WIDE), F32)
     halves = pltpu.VMEM((2, 7, HALF, WIDE), BF)
     block = pltpu.VMEM((GROUPS * PAD, WIDE), BF)
-    out = jax.ShapeDtypeStruct((TOK, TOK), BF)
-    return pl.pallas_call(
+    both = pl.pallas_call(
         kernel,
-        out_shape=(out, out),
+        out_shape=jax.ShapeDtypeStruct((2, TOK, TOK), BF),
         in_specs=[hbm] * 7,
-        out_specs=(vm, vm),
+        out_specs=vm,
         scratch_shapes=[
             pltpu.VMEM((TOK, TOK), BF), pltpu.VMEM((TOK, TOK), BF),
             pltpu.VMEM((2, TOK), jnp.int32), pltpu.VMEM((2, TOK), F32), dma((4,)),
@@ -378,6 +380,7 @@
         tokens, cotangent, routes.T, route_weight.T,
         w_gate.reshape(SIDE, SIDE, TOK, HID), w_up.reshape(SIDE, SIDE, TOK, HID), w_down[0],
     )
+    return both[0], both[1]
 
 
 def solution(mesh):

time: 73.1 us -> 71.2 us (0.974)
  local copies, waits for them, and re-layouts: 2.61 us -> 1.33 us
    unnamed x2 -> x0, local copies, waits for them, and re-layouts: 2.61 us -> none
    squeeze x0 -> x1, local copies, waits for them, and re-layouts: none -> 1.33 us  [shards(): return (both[0], both[1])]
where the time goes in v4:
time: 71.2 us; the launch traced here: 70.9 us
  Pallas kernels  69 us (97%)
  local copies, waits for them, and re-layouts  1.33 us (2%)
    pallas_call x1, Pallas kernels, shards(): pl.pallas_call(kernel, out_shape=jax.ShapeDtypeStruct((2, TOK, TOK), BF),...  69 us

profile of v4, /device:TPU:1, one launch (start us, length us, event | category | flops | bytes accessed | tf_op | source)
XLA Modules:
  0.0 70.9 jit_solution(12520758719018678919)
XLA Ops:
  0.6 69.0 %moe.1 = bf16[2,48,48]{2,1,0:T(8,128)(2,1)} custom-call(bf16[48,48]{1,0:T(8,128)(2,1)} %tok_h.1, bf16[48,48]{1,0:T(8,128)(2,1)} %cot_h.1, s32[2,48]{1,0:T(2,128)} %bitcast.12, f32[2,48]{1,0:T(2,128)} %bitcast.13, bf16[8,8,48,256]{3,2,1,0:T(8,128)(2,1)} %bitcast.9, bf16[8,8,48,256]{3,2,1,0:T(8,128)(2,1)} %bitcast.10, bf16[256,3072]{1,0:T(8,128)(2,1)} %bitcast.11), custom_call_target="tpu_custom_call" | custom-call | tf_op jit(solution)/shard_map/moe/pallas_call | solution.py:355
  69.6 1.3 %slice_bitcast_fusion = (bf16[48,48]{1,0:T(8,128)(2,1)}, bf16[48,48]{1,0:T(8,128)(2,1)}) fusion(bf16[2,48,48]{2,1,0:T(8,128)(2,1)} %moe.1), kind=kLoop, calls=%fused_computation | loop fusion | bytes 18432 | tf_op jit(solution)/shard_map/squeeze | solution.py:383

commit v5 on v4

--- a/solution.py
+++ b/solution.py
@@ -51,7 +51,7 @@
     tok_h, cot_h, routes_h, rw_h, wg, wu, wd,
     out_ref,
     tok, cot, routes, rw, isem,
-    wgu, wdv, spread, comp, dsend, drecv, rsend, rrecv,
+    wgu, wdv, comp, dsend, drecv, rsend, rrecv,
     t1, g1, t2, g2, pm, pg, ms, gs, mr, gr, mp, gp, mq, gq,
     wsem, s1, r1, ds_, dr, s2, r2, s3, r3, rs_, rr, s4, r4,
 ):
@@ -129,10 +129,6 @@
     m1 = onehot(slot == p1)
     n0 = onehot(slot == p0 + CAP)
     n1 = onehot(slot == p1 + CAP)
-    l_ = iota((LANES, WIDE), 0)
-    c_ = iota((LANES, WIDE), 1)
-    for k in range(SIDE):
-        spread[pl.ds(k * LANES, LANES), :] = onehot((c_ - l_ == TOK * k) & (l_ < TOK))
     q_ = iota((HALF, GROUPS // 2 * PAD), 1)
     s_ = iota((HALF, GROUPS // 2 * PAD), 0)
     group = ((q_.astype(F32) + 0.5) * (1.0 / PAD)).astype(jnp.int32)
@@ -140,8 +136,21 @@
     row = group * CAP + place
     comp[pl.ds(0, HALF), :] = onehot((row == s_) & (place < CAP))
     comp[pl.ds(HALF, HALF), :] = onehot((row == s_ + CAP) & (place >= CAP) & (place < 2 * CAP))
+    starts = [divmod(TOK * k, LANES) for k in range(SIDE)]
+
+    def turn(block, r):
+        return pltpu.roll(block, r, 1) if r else block
+
     def unpack(ref):
-        return mm(jnp.concatenate([ref[k] for k in range(SIDE)], axis=1), spread[...])
+        tiles = [0.0] * (WIDE // LANES)
+        for k, (j, r) in enumerate(starts):
+            block = turn(ref[k].astype(F32), r)
+            if r + TOK <= LANES:
+                tiles[j] += block
+            else:
+                tiles[j] += jnp.where(lane >= r, block, 0.0)
+                tiles[j + 1] += jnp.where(lane < r + TOK - LANES, block, 0.0)
+        return jnp.concatenate(tiles, axis=1)
 
     for c in copies[0::2]:
         c.wait_recv()
@@ -296,10 +305,11 @@
     use(0, 0)
     pass_on(0)
     one(1)
-    use(0, 2, 6)
+    use(0, 2)
+    pass_on(1)
+    use(0, 6)
     arrived(0, 2, 3)
     use(0, 1, 7)
-    pass_on(1)
     arrived(0, 4, 5, 6)
     use(0, 3, 5, 4)
     activate(0)
@@ -307,8 +317,8 @@
     use(1, 0, 2, 6)
     arrived(1, 2, 3)
     use(1, 1, 7)
+    arrived(1, 4, 5, 6)
     middle_sums(0)
-    arrived(1, 4, 5, 6)
     use(1, 3, 5, 4)
     activate(1)
     start_sums(1)
@@ -322,13 +332,16 @@
     back = rrecv[...]
 
     def spread_out(values, buf):
-        flat = mm_nt(values, spread[...]).astype(BF)
-        for k in range(SIDE):
-            buf[k] = flat[:, k * LANES:(k + 1) * LANES]
-
-    spread_out((w0 * mm(m0, back) + w1 * mm(m1, back)).astype(BF), mp)
+        for k, (j, r) in enumerate(starts):
+            block = turn(values[:, j * LANES:(j + 1) * LANES], (LANES - r) % LANES)
+            if r + TOK > LANES:
+                after = turn(values[:, (j + 1) * LANES:(j + 2) * LANES], LANES - r)
+                block = jnp.where(lane < LANES - r, block, after)
+            buf[k] = block.astype(BF)
+
+    spread_out(w0 * mm(m0, back) + w1 * mm(m1, back), mp)
     last = [send(mp.at[(z + d) % SIDE], mq.at[d], s4.at[0, d], r4.at[0, d], at_z(d)) for d in FAR]
-    spread_out(mm(n0 + n1, back).astype(BF), gp)
+    spread_out(mm(n0 + n1, back), gp)
     last += [send(gp.at[(y + d) % SIDE], gq.at[d], s4.at[1, d], r4.at[1, d], at_y(d)) for d in FAR]
     mtot = mp[z].astype(F32)
     gtot = gp[y].astype(F32)
@@ -362,7 +375,6 @@
             pltpu.VMEM((2, TOK), jnp.int32), pltpu.VMEM((2, TOK), F32), dma((4,)),
             pltpu.VMEM((SIDE, SIDE, TOK, 2 * HID), BF),
             pltpu.VMEM((HID, SIDE * WIDE), BF),
-            pltpu.VMEM((SIDE * LANES, WIDE), BF),
             pltpu.VMEM((ROWS, GROUPS // 2 * PAD), BF),
             block, block, block, block,
             small, small, big, big, tall, tall,

time: 71.2 us -> 70.7 us (level)
  no operation moved by 1% of the time
where the time goes in v5:
time: 70.7 us; the launch traced here: 70.4 us
  Pallas kernels  68.5 us (97%)
  local copies, waits for them, and re-layouts  1.33 us (2%)
    pallas_call x1, Pallas kernels, shards(): pl.pallas_call(kernel, out_shape=jax.ShapeDtypeStruct((2, TOK, TOK), BF),...  68.5 us

profile of v5, /device:TPU:1, one launch (start us, length us, event | category | flops | bytes accessed | tf_op | source)
XLA Modules:
  0.0 70.4 jit_solution(14107189283270607949)
XLA Ops:
  0.6 68.5 %moe.1 = bf16[2,48,48]{2,1,0:T(8,128)(2,1)} custom-call(bf16[48,48]{1,0:T(8,128)(2,1)} %tok_h.1, bf16[48,48]{1,0:T(8,128)(2,1)} %cot_h.1, s32[2,48]{1,0:T(2,128)} %bitcast.12, f32[2,48]{1,0:T(2,128)} %bitcast.13, bf16[8,8,48,256]{3,2,1,0:T(8,128)(2,1)} %bitcast.9, bf16[8,8,48,256]{3,2,1,0:T(8,128)(2,1)} %bitcast.10, bf16[256,3072]{1,0:T(8,128)(2,1)} %bitcast.11), custom_call_target="tpu_custom_call" | custom-call | tf_op jit(solution)/shard_map/moe/pallas_call | solution.py:368
  69.1 1.3 %slice_bitcast_fusion = (bf16[48,48]{1,0:T(8,128)(2,1)}, bf16[48,48]{1,0:T(8,128)(2,1)}) fusion(bf16[2,48,48]{2,1,0:T(8,128)(2,1)} %moe.1), kind=kLoop, calls=%fused_computation | loop fusion | bytes 18432 | tf_op jit(solution)/shard_map/squeeze | solution.py:395

commit v6 on v5

--- a/solution.py
+++ b/solution.py
@@ -322,8 +322,8 @@
     use(1, 3, 5, 4)
     activate(1)
     start_sums(1)
+    middle_sums(1)
     end_sums(0)
-    middle_sums(1)
     end_sums(1)
     for c in (*copies.values(), *moves.values(), *hops.values()):
         c.wait_send()

time: 70.7 us -> 70.7 us (level)
  no operation moved by 1% of the time
where the time goes in v6:
time: 70.7 us; the launch traced here: 70.4 us
  Pallas kernels  68.4 us (97%)
  local copies, waits for them, and re-layouts  1.33 us (2%)
    pallas_call x1, Pallas kernels, shards(): pl.pallas_call(kernel, out_shape=jax.ShapeDtypeStruct((2, TOK, TOK), BF),...  68.4 us

profile of v6, /device:TPU:1, one launch (start us, length us, event | category | flops | bytes accessed | tf_op | source)
XLA Modules:
  0.0 70.4 jit_solution(12178263180900934036)
XLA Ops:
  0.6 68.4 %moe.1 = bf16[2,48,48]{2,1,0:T(8,128)(2,1)} custom-call(bf16[48,48]{1,0:T(8,128)(2,1)} %tok_h.1, bf16[48,48]{1,0:T(8,128)(2,1)} %cot_h.1, s32[2,48]{1,0:T(2,128)} %bitcast.12, f32[2,48]{1,0:T(2,128)} %bitcast.13, bf16[8,8,48,256]{3,2,1,0:T(8,128)(2,1)} %bitcast.9, bf16[8,8,48,256]{3,2,1,0:T(8,128)(2,1)} %bitcast.10, bf16[256,3072]{1,0:T(8,128)(2,1)} %bitcast.11), custom_call_target="tpu_custom_call" | custom-call | tf_op jit(solution)/shard_map/moe/pallas_call | solution.py:368
  69.1 1.3 %slice_bitcast_fusion = (bf16[48,48]{1,0:T(8,128)(2,1)}, bf16[48,48]{1,0:T(8,128)(2,1)}) fusion(bf16[2,48,48]{2,1,0:T(8,128)(2,1)} %moe.1), kind=kLoop, calls=%fused_computation | loop fusion | bytes 18432 | tf_op jit(solution)/shard_map/squeeze | solution.py:395
